TPU v7x, 32 devices: a whole 2x2x4 slice. The times are simulated.
32 devices in a mesh: dp: 4 (over y, x), expert: 8 (over z, core).
Axes of the slice: x: 2, y: 2, z: 4, core: 2. Of those that a mesh axis runs over, the one named last changes fastest.
Arguments:
- output_grad: bfloat16 [6144, 2048], P(('dp', 'expert')), may hold values from -3 to 3
- routes: int32 [6144, 2], P(('dp', 'expert')), may hold values from 0 to 7, all different within a row; in each aligned block of 192 rows (0 to 191, 192 to 383, ...) at most 72 rows name the same one
- combine_weights: bfloat16 [6144, 2], P(('dp', 'expert')), may hold values from 0.049804688 to 0.5
- saved_hidden: bfloat16 [18432, 768], P(('dp', 'expert')), may hold values from -0.796875 to 0.796875
- down_weight: bfloat16 [8, 768, 2048], P('expert', 'dp'), may hold values from -0.21875 to 0.21875
Outputs:
- hidden_grad: bfloat16 [18432, 768], P(('dp', 'expert'))
- weight_grad: float32 [8, 768, 2048], P('expert', 'dp')
- route_grad: float32 [6144, 2], P(('dp', 'expert'))
Inputs may be any that keep to these rules, and one draw needn't show every extreme that they name: Each token names 2 different experts; among the 192 rows of one device no expert is named by more than 72 routes.
All inputs are finite; a program needn't handle non-finite values.
Results may differ from a plain program's by a relative error of at most 0.008.
Values may be sent and summed in bfloat16 or wider, within the bound.
A program may use at most 64 MiB of HBM per device.

v0:
```python
import jax
import jax.numpy as jnp
from jax import lax
from jax.sharding import PartitionSpec as P


def route_slots(routes, experts, capacity):
    flat_ids = routes.reshape(-1)
    one_hot = (flat_ids[:, None] == jnp.arange(experts, dtype=jnp.int32)[None, :]).astype(jnp.int32)
    earlier = jnp.cumsum(one_hot, axis=0) - one_hot
    return flat_ids * capacity + jnp.sum(earlier * one_hot, axis=1)


def per_device(output_grad, routes, combine_weights, saved_hidden, down_weight):
    experts = lax.axis_size("expert")
    slot_count = saved_hidden.shape[0]
    capacity = slot_count // experts
    features = output_grad.shape[1]
    route_total = routes.shape[0] * routes.shape[1]
    target = route_slots(routes, experts, capacity)
    source = (
        jnp.full((slot_count,), route_total, jnp.int32)
        .at[target]
        .set(jnp.arange(route_total, dtype=jnp.int32))
    )
    is_live = source < route_total
    safe_index = jnp.where(is_live, source, 0)
    send_rows = jnp.where(
        is_live[:, None], output_grad[safe_index // routes.shape[1]], jnp.zeros((), jnp.bfloat16)
    )
    send_weights = jnp.where(
        is_live, combine_weights.reshape(-1)[safe_index], jnp.zeros((), jnp.bfloat16)
    )
    recv_rows, recv_weights = (
        lax.all_to_all(
            send_rows.reshape(experts, capacity, features),
            "expert",
            split_axis=0,
            concat_axis=0,
            tiled=True,
        ),
        lax.all_to_all(
            send_weights.reshape(experts, capacity),
            "expert",
            split_axis=0,
            concat_axis=0,
            tiled=True,
        ),
    )
    grad_rows = recv_rows.reshape(slot_count, features)
    slot_weights = recv_weights.reshape(slot_count).astype(jnp.float32)
    weighted = (slot_weights[:, None] * grad_rows.astype(jnp.float32)).astype(jnp.bfloat16)
    weight_shard = down_weight[0]
    contract = (((1,), (1,)), ((), ()))
    full_weight = lax.all_gather(weight_shard, "dp", axis=0, tiled=True)
    unscaled = lax.dot_general(grad_rows, full_weight, contract, preferred_element_type=jnp.float32)
    route_terms = jnp.sum(saved_hidden.astype(jnp.float32) * unscaled, axis=1)
    hidden_grad = (slot_weights[:, None] * unscaled).astype(jnp.bfloat16)
    grad_part = lax.psum_scatter(
        lax.dot_general(
            saved_hidden, weighted, (((0,), (0,)), ((), ())), preferred_element_type=jnp.float32
        ).astype(jnp.bfloat16),
        "dp",
        scatter_dimension=0,
        tiled=True,
    ).astype(jnp.float32)
    returned = lax.all_to_all(
        route_terms.reshape(experts, capacity), "expert", split_axis=0, concat_axis=0, tiled=True
    )
    route_grad = returned.reshape(-1)[target].reshape(routes.shape)
    return (hidden_grad, grad_part[None], route_grad)


def solution(mesh):
    return jax.shard_map(
        per_device,
        mesh=mesh,
        in_specs=(
            P(("dp", "expert"), None),
            P(("dp", "expert"), None),
            P(("dp", "expert"), None),
            P(("dp", "expert"), None),
            P("expert", "dp", None),
        ),
        out_specs=(P(("dp", "expert"), None), P("expert", "dp", None), P(("dp", "expert"), None)),
        check_vma=False,
    )
```

profile of v0, /device:TPU:11, one launch (start us, length us, event | category | flops | bytes accessed | tf_op | source)
XLA Modules:
  0.0 155.0 jit_solution(16098599032661356121)
XLA Ops:
  7.2 0.9 copy.16
  8.3 0.7 broadcast_multiply_fusion
  9.0 0.8 reduce-window.6
  10.5 2.9 %scatter_custom_fusion = s32[576]{0:T(1024)S(1)} fusion(s32[384]{0:T(512)S(1)} %fusion.11, s32[384]{0:T(512)S(1)} %iota.11, s32[]{:T(128)} %constant.12.clone.1), kind=kCustom, calls=%fused_computation.36 | custom fusion | bytes 2308 | tf_op jit(solution)/shard_map/scatter | solution.py:24
  13.5 0.8 copy.18
  14.5 3.9 %gather_fusion = bf16[576]{0:T(1024)(128)(2,1)S(1)} fusion(bf16[384]{0:T(512)(128)(2,1)S(1)} %reshape.91, s32[1024]{0:T(1024)S(1)} %pad_clamp_fusion.2), kind=kCustom, calls=%fused_computation | custom fusion | bytes 4608 | tf_op jit(solution)/shard_map/gather | solution.py:32
  18.5 0.7 all_to_all.20
  19.1 5.6 %all-to-all-start = ((bf16[8,1,72]{2,1,0:T(2,128)(2,1)}), bf16[8,1,72]{2,1,0:T(2,128)(2,1)S(1)}, u32[]{:S(2)}, u32[]{:S(2)}) async-start(bf16[8,1,72]{2,1,0:T(2,128)(2,1)} %all_to_all.20), calls=%async_computation | async-start | bytes 8192 | tf_op jit(solution)/shard_map/all_to_all | solution.py:42
  24.8 0.7 all-gather.3.cloned.1.call-update
  25.6 3.4 %gather_fusion.1 = bf16[576,2048]{1,0:T(8,128)(2,1)S(1)} fusion(bf16[192,2048]{1,0:T(8,128)(2,1)S(1)} %copy-done, s32[1024]{0:T(1024)S(1)} %pad_clamp_fusion.1), kind=kCustom, calls=%fused_computation.1 | custom fusion | bytes 4720896 | tf_op jit(solution)/shard_map/gather | solution.py:29
  29.0 1.7 %broadcast_select_fusion = bf16[8,72,2048]{2,1,0:T(8,128)(2,1)} fusion(bf16[8,72,2048]{2,1,0:T(8,128)(2,1)S(1)} %bitcast.24, pred[8,72]{1,0:T(8,128)(4,1)S(1)} %broadcast_in_dim.43), kind=kLoop, calls=%fused_computation.10 | loop fusion | flops 1179648 | bytes 4719168 | tf_op jit(solution)/shard_map/jit(_where)/select_n | solution.py:28
  30.7 5.1 %all-to-all-start.1 = ((bf16[8,72,2048]{2,1,0:T(8,128)(2,1)}), bf16[8,72,2048]{2,1,0:T(8,128)(2,1)S(1)}, u32[]{:S(2)}, u32[]{:S(2)}) async-start(bf16[8,72,2048]{2,1,0:T(8,128)(2,1)} %broadcast_select_fusion), calls=%async_computation.1 | async-start | bytes 4718592 | tf_op jit(solution)/shard_map/all_to_all | solution.py:35
  35.9 51.0 %all-to-all-done.1 = bf16[8,72,2048]{2,1,0:T(8,128)(2,1)S(1)} async-done(((bf16[8,72,2048]{2,1,0:T(8,128)(2,1)}), bf16[8,72,2048]{2,1,0:T(8,128)(2,1)S(1)}, u32[]{:S(2)}, u32[]{:S(2)}) %all-to-all-start.1) | async-done | bytes 2359328 | tf_op jit(solution)/shard_map/all_to_all | solution.py:35
  86.9 5.5 %fusion.2 = bf16[768,2048]{0,1:T(8,128)(2,1)} fusion(bf16[576,768]{1,0:T(8,128)(2,1)} %param.8, bf16[576,2048]{1,0:T(8,128)(2,1)S(1)} %bitcast.25, f32[576]{0:T(1024)S(1)} %reshape.95), kind=kOutput, calls=%fused_computation.8 | convolution fusion | flops 1817051136 | bytes 6392064 | tf_op jit(solution)/shard_map/dot_general | solution.py:60
  92.5 4.7 %copy.22 = bf16[768,2048]{1,0:T(8,128)(2,1)} copy(bf16[768,2048]{0,1:T(8,128)(2,1)} %fusion.2) | data formatting | bytes 6291456
  97.2 5.1 %multiply_reduce_fusion = (f32[576]{0:T(1024)S(1)}, bf16[576,768]{1,0:T(8,128)(2,1)}) fusion(bf16[576,768]{1,0:T(8,128)(2,1)} %param.8, f32[576]{0:T(1024)S(1)} %reshape.95, bf16[576,2048]{1,0:T(8,128)(2,1)S(1)} %bitcast.26, bf16[1,768,2048]{2,1,0:T(8,128)(2,1)} %all-gather.3.cloned.1.call-done), kind=kOutput, calls=%fused_computation.11 | convolution fusion | flops 1814150656 | bytes 7279104 | tf_op jit(solution)/shard_map/dot_general | solution.py:56
  102.3 0.7 all_to_all.18
  103.0 6.8 %all-to-all-start.2 = ((f32[8,1,72]{2,1,0:T(1,128)}), f32[8,1,72]{2,1,0:T(1,128)S(1)}, u32[]{:S(2)}, u32[]{:S(2)}) async-start(f32[8,1,72]{2,1,0:T(1,128)} %all_to_all.18), calls=%async_computation.2 | async-start | bytes 8192 | tf_op jit(solution)/shard_map/all_to_all | solution.py:67
  109.8 3.8 %all-to-all-done.2 = f32[8,1,72]{2,1,0:T(1,128)S(1)} async-done(((f32[8,1,72]{2,1,0:T(1,128)}), f32[8,1,72]{2,1,0:T(1,128)S(1)}, u32[]{:S(2)}, u32[]{:S(2)}) %all-to-all-start.2) | async-done | bytes 2336 | tf_op jit(solution)/shard_map/all_to_all | solution.py:67
  114.8 1.9 %gather_fusion.2 = f32[384]{0:T(512)S(1)} fusion(f32[576]{0:T(1024)S(1)} %reshape.93, s32[1024]{0:T(1024)S(1)} %pad_clamp_fusion), kind=kCustom, calls=%fused_computation.2 | custom fusion | bytes 4608 | tf_op jit(solution)/shard_map/gather | solution.py:70
  117.5 25.3 %reduce-scatter.4.cloned.1.call-done = bf16[192,2048]{1,0:T(8,128)(2,1)} async-done(((bf16[768,2048]{1,0:T(8,128)(2,1)}), bf16[192,2048]{1,0:T(8,128)(2,1)}) %reduce-scatter.4.cloned.1.call-update) | async-done | bytes 786448
  142.8 2.2 %copy.23 = bf16[192,2048]{0,1:T(8,128)(2,1)} copy(bf16[192,2048]{1,0:T(8,128)(2,1)} %reduce-scatter.4.cloned.1.call-done) | data formatting | bytes 1572864
  145.0 1.4 bitcast_convert_fusion
  146.4 1.7 %copy.20 = f32[1,192,2048]{2,1,0:T(8,128)} copy(f32[1,192,2048]{1,2,0:T(8,128)S(1)} %bitcast_convert_fusion) | data formatting | bytes 3145728
  (32 shorter events, 3.4 us)
Async XLA Ops:
  7.2 18.4 %copy-start = (bf16[192,2048]{1,0:T(8,128)(2,1)S(1)}, bf16[192,2048]{1,0:T(8,128)(2,1)}, u32[]{:S(2)}) copy-start(bf16[192,2048]{1,0:T(8,128)(2,1)} %param.5) | copy-start | bytes 2359300
  19.1 11.6 %all-to-all-start = ((bf16[8,1,72]{2,1,0:T(2,128)(2,1)}), bf16[8,1,72]{2,1,0:T(2,128)(2,1)S(1)}, u32[]{:S(2)}, u32[]{:S(2)}) async-start(bf16[8,1,72]{2,1,0:T(2,128)(2,1)} %all_to_all.20), calls=%async_computation | async-start | bytes 8192 | tf_op jit(solution)/shard_map/all_to_all | solution.py:42
  24.8 72.4 %all-gather.3.cloned.1.call-start = ((), (), s32[]{:S(2)}) async-start(), calls=%async_computation.4 | async-start | bytes 3932160 | tf_op jit(solution)/shard_map/all_gather | solution.py:55
  30.7 56.2 %all-to-all-start.1 = ((bf16[8,72,2048]{2,1,0:T(8,128)(2,1)}), bf16[8,72,2048]{2,1,0:T(8,128)(2,1)S(1)}, u32[]{:S(2)}, u32[]{:S(2)}) async-start(bf16[8,72,2048]{2,1,0:T(8,128)(2,1)} %broadcast_select_fusion), calls=%async_computation.1 | async-start | bytes 4718592 | tf_op jit(solution)/shard_map/all_to_all | solution.py:35
  35.8 107.0 %reduce-scatter.4.cloned.1.call-start = ((), (), s32[]{:S(2)}) async-start(), calls=%async_computation.5 | async-start | bytes 3932160
  103.0 10.6 %all-to-all-start.2 = ((f32[8,1,72]{2,1,0:T(1,128)}), f32[8,1,72]{2,1,0:T(1,128)S(1)}, u32[]{:S(2)}, u32[]{:S(2)}) async-start(f32[8,1,72]{2,1,0:T(1,128)} %all_to_all.18), calls=%async_computation.2 | async-start | bytes 8192 | tf_op jit(solution)/shard_map/all_to_all | solution.py:67
Sparse Core Ops, SparseCore 0:
  27.4 44.5 all-gather.2
  97.3 45.4 reduce-scatter.3
where the time goes:
time: 157 us; the launch traced here: 155 us
  waiting for transfers between devices  80.9 us (52%)
  local copies, waits for them, and re-layouts  26.3 us (17%)
  starting transfers between devices  17.5 us (11%)
  between operations  14.2 us (9%)
  matrix products  10.6 us (7%)
  other arithmetic  5.47 us (3%)
    all_to_all x1, waiting for transfers between devices, per_device(): lax.all_to_all(send_rows.reshape(experts, capacity, features), 'expert',...  51 us
    unnamed x3, waiting for transfers between devices  26 us
    unnamed x8, local copies, waits for them, and re-layouts  11 us
    all_to_all x1, starting transfers between devices, per_device(): lax.all_to_all(route_terms.reshape(experts, capacity), 'expert', split_ax...  6.78 us
    all_to_all x1, starting transfers between devices, per_device(): lax.all_to_all(send_weights.reshape(experts, capacity), 'expert', split_a...  5.64 us
    dot_general x1, matrix products, per_device(): lax.dot_general(saved_hidden, weighted, (((0,), (0,)), ((), ())), preferr...  5.53 us
    all_to_all x1, starting transfers between devices, per_device(): lax.all_to_all(send_rows.reshape(experts, capacity, features), 'expert',...  5.1 us
    dot_general x1, matrix products, per_device(): lax.dot_general(grad_rows, full_weight, contract, preferred_element_type=...  5.08 us
  transfers between devices with their start and end apart: 5, of which 3 were waited for; matrix products, arithmetic and copies ran while one was open for 16% of the time, Pallas kernels for 0%

commit v1 on v0

--- a/solution.py
+++ b/solution.py
@@ -6,9 +6,10 @@
 
 def route_slots(routes, experts, capacity):
     flat_ids = routes.reshape(-1)
-    one_hot = (flat_ids[:, None] == jnp.arange(experts, dtype=jnp.int32)[None, :]).astype(jnp.int32)
-    earlier = jnp.cumsum(one_hot, axis=0) - one_hot
-    return flat_ids * capacity + jnp.sum(earlier * one_hot, axis=1)
+    place = jnp.arange(flat_ids.shape[0], dtype=jnp.int32)
+    same = flat_ids[:, None] == flat_ids[None, :]
+    rank = jnp.sum((same & (place[None, :] < place[:, None])).astype(jnp.int32), axis=1)
+    return flat_ids * capacity + rank
 
 
 def per_device(output_grad, routes, combine_weights, saved_hidden, down_weight):

time: 157 us -> 156 us (level)
  no operation moved by 1% of the time
where the time goes in v1:
time: 156 us; the launch traced here: 154 us
  waiting for transfers between devices  80.9 us (52%)
  local copies, waits for them, and re-layouts  25.9 us (17%)
  starting transfers between devices  17.5 us (11%)
  between operations  14.2 us (9%)
  matrix products  10.6 us (7%)
  other arithmetic  4.72 us (3%)
    all_to_all x1, waiting for transfers between devices, per_device(): lax.all_to_all(send_rows.reshape(experts, capacity, features), 'expert',...  51 us
    unnamed x3, waiting for transfers between devices  26 us
    unnamed x8, local copies, waits for them, and re-layouts  11 us
    all_to_all x1, starting transfers between devices, per_device(): lax.all_to_all(route_terms.reshape(experts, capacity), 'expert', split_ax...  6.78 us
    all_to_all x1, starting transfers between devices, per_device(): lax.all_to_all(send_weights.reshape(experts, capacity), 'expert', split_a...  5.64 us
    dot_general x1, matrix products, per_device(): lax.dot_general(saved_hidden, weighted, (((0,), (0,)), ((), ())), preferr...  5.51 us
    all_to_all x1, starting transfers between devices, per_device(): lax.all_to_all(send_rows.reshape(experts, capacity, features), 'expert',...  5.1 us
    dot_general x1, matrix products, per_device(): lax.dot_general(grad_rows, full_weight, contract, preferred_element_type=...  5.08 us
  transfers between devices with their start and end apart: 5, of which 3 were waited for; matrix products, arithmetic and copies ran while one was open for 16% of the time, Pallas kernels for 0%

profile of v1, /device:TPU:11, one launch (start us, length us, event | category | flops | bytes accessed | tf_op | source)
XLA Modules:
  0.0 153.8 jit_solution(9721528789717610883)
XLA Ops:
  7.2 0.9 copy.21
  8.1 0.7 broadcast_multiply_fusion
  9.4 2.9 %scatter_custom_fusion = s32[576]{0:T(1024)S(1)} fusion(s32[384]{0:T(512)S(1)} %fusion.9, s32[384]{0:T(512)S(1)} %iota.10, s32[]{:T(128)} %constant.9.clone.1), kind=kCustom, calls=%fused_computation.32 | custom fusion | bytes 2308 | tf_op jit(solution)/shard_map/scatter | solution.py:25
  12.4 0.8 copy.22
  13.4 3.9 %gather_fusion = bf16[576]{0:T(1024)(128)(2,1)S(1)} fusion(bf16[384]{0:T(512)(128)(2,1)S(1)} %reshape.75, s32[1024]{0:T(1024)S(1)} %pad_clamp_fusion.2), kind=kCustom, calls=%fused_computation | custom fusion | bytes 4608 | tf_op jit(solution)/shard_map/gather | solution.py:33
  17.3 0.7 all_to_all.20
  18.0 5.6 %all-to-all-start = ((bf16[8,1,72]{2,1,0:T(2,128)(2,1)}), bf16[8,1,72]{2,1,0:T(2,128)(2,1)S(1)}, u32[]{:S(2)}, u32[]{:S(2)}) async-start(bf16[8,1,72]{2,1,0:T(2,128)(2,1)} %all_to_all.20), calls=%async_computation | async-start | bytes 8192 | tf_op jit(solution)/shard_map/all_to_all | solution.py:43
  23.7 0.7 all-gather.3.cloned.1.call-update
  24.5 3.4 %gather_fusion.1 = bf16[576,2048]{1,0:T(8,128)(2,1)S(1)} fusion(bf16[192,2048]{1,0:T(8,128)(2,1)S(1)} %copy-done, s32[1024]{0:T(1024)S(1)} %pad_clamp_fusion.1), kind=kCustom, calls=%fused_computation.1 | custom fusion | bytes 4720896 | tf_op jit(solution)/shard_map/gather | solution.py:30
  27.9 1.7 %broadcast_select_fusion = bf16[8,72,2048]{2,1,0:T(8,128)(2,1)} fusion(bf16[8,72,2048]{2,1,0:T(8,128)(2,1)S(1)} %bitcast.15, pred[8,72]{1,0:T(8,128)(4,1)S(1)} %broadcast_in_dim.44), kind=kLoop, calls=%fused_computation.10 | loop fusion | flops 1179648 | bytes 4719168 | tf_op jit(solution)/shard_map/jit(_where)/select_n | solution.py:29
  29.6 5.1 %all-to-all-start.1 = ((bf16[8,72,2048]{2,1,0:T(8,128)(2,1)}), bf16[8,72,2048]{2,1,0:T(8,128)(2,1)S(1)}, u32[]{:S(2)}, u32[]{:S(2)}) async-start(bf16[8,72,2048]{2,1,0:T(8,128)(2,1)} %broadcast_select_fusion), calls=%async_computation.1 | async-start | bytes 4718592 | tf_op jit(solution)/shard_map/all_to_all | solution.py:36
  34.8 51.0 %all-to-all-done.1 = bf16[8,72,2048]{2,1,0:T(8,128)(2,1)S(1)} async-done(((bf16[8,72,2048]{2,1,0:T(8,128)(2,1)}), bf16[8,72,2048]{2,1,0:T(8,128)(2,1)S(1)}, u32[]{:S(2)}, u32[]{:S(2)}) %all-to-all-start.1) | async-done | bytes 2359328 | tf_op jit(solution)/shard_map/all_to_all | solution.py:36
  85.8 5.5 %fusion.2 = bf16[768,2048]{0,1:T(8,128)(2,1)} fusion(bf16[576,768]{1,0:T(8,128)(2,1)} %param.8, bf16[576,2048]{1,0:T(8,128)(2,1)S(1)} %bitcast.16, f32[576]{0:T(1024)S(1)} %reshape.79), kind=kOutput, calls=%fused_computation.8 | convolution fusion | flops 1817051136 | bytes 6392064 | tf_op jit(solution)/shard_map/dot_general | solution.py:61
  91.3 4.7 %copy.26 = bf16[768,2048]{1,0:T(8,128)(2,1)} copy(bf16[768,2048]{0,1:T(8,128)(2,1)} %fusion.2) | data formatting | bytes 6291456
  96.1 5.1 %multiply_reduce_fusion = (f32[576]{0:T(1024)S(1)}, bf16[576,768]{1,0:T(8,128)(2,1)}) fusion(bf16[576,768]{1,0:T(8,128)(2,1)} %param.8, f32[576]{0:T(1024)S(1)} %reshape.79, bf16[576,2048]{1,0:T(8,128)(2,1)S(1)} %bitcast.17, bf16[1,768,2048]{2,1,0:T(8,128)(2,1)} %all-gather.3.cloned.1.call-done), kind=kOutput, calls=%fused_computation.11 | convolution fusion | flops 1814150656 | bytes 7279104 | tf_op jit(solution)/shard_map/dot_general | solution.py:57
  101.2 0.7 all_to_all.18
  101.9 6.8 %all-to-all-start.2 = ((f32[8,1,72]{2,1,0:T(1,128)}), f32[8,1,72]{2,1,0:T(1,128)S(1)}, u32[]{:S(2)}, u32[]{:S(2)}) async-start(f32[8,1,72]{2,1,0:T(1,128)} %all_to_all.18), calls=%async_computation.2 | async-start | bytes 8192 | tf_op jit(solution)/shard_map/all_to_all | solution.py:68
  108.6 3.8 %all-to-all-done.2 = f32[8,1,72]{2,1,0:T(1,128)S(1)} async-done(((f32[8,1,72]{2,1,0:T(1,128)}), f32[8,1,72]{2,1,0:T(1,128)S(1)}, u32[]{:S(2)}, u32[]{:S(2)}) %all-to-all-start.2) | async-done | bytes 2336 | tf_op jit(solution)/shard_map/all_to_all | solution.py:68
  112.9 0.7 reduce.9
  113.7 1.9 %gather_fusion.2 = f32[384]{0:T(512)S(1)} fusion(f32[576]{0:T(1024)S(1)} %reshape.77, s32[1024]{0:T(1024)S(1)} %pad_clamp_fusion), kind=kCustom, calls=%fused_computation.2 | custom fusion | bytes 4608 | tf_op jit(solution)/shard_map/gather | solution.py:71
  116.4 25.3 %reduce-scatter.4.cloned.1.call-done = bf16[192,2048]{1,0:T(8,128)(2,1)} async-done(((bf16[768,2048]{1,0:T(8,128)(2,1)}), bf16[192,2048]{1,0:T(8,128)(2,1)}) %reduce-scatter.4.cloned.1.call-update) | async-done | bytes 786448
  141.7 2.2 %copy.27 = bf16[192,2048]{0,1:T(8,128)(2,1)} copy(bf16[192,2048]{1,0:T(8,128)(2,1)} %reduce-scatter.4.cloned.1.call-done) | data formatting | bytes 1572864
  143.9 1.4 bitcast_convert_fusion
  145.3 1.7 %copy.24 = f32[1,192,2048]{2,1,0:T(8,128)} copy(f32[1,192,2048]{1,2,0:T(8,128)S(1)} %bitcast_convert_fusion) | data formatting | bytes 3145728
  (27 shorter events, 2.5 us)
Async XLA Ops:
  7.2 17.3 %copy-start = (bf16[192,2048]{1,0:T(8,128)(2,1)S(1)}, bf16[192,2048]{1,0:T(8,128)(2,1)}, u32[]{:S(2)}) copy-start(bf16[192,2048]{1,0:T(8,128)(2,1)} %param.5) | copy-start | bytes 2359300
  18.0 11.6 %all-to-all-start = ((bf16[8,1,72]{2,1,0:T(2,128)(2,1)}), bf16[8,1,72]{2,1,0:T(2,128)(2,1)S(1)}, u32[]{:S(2)}, u32[]{:S(2)}) async-start(bf16[8,1,72]{2,1,0:T(2,128)(2,1)} %all_to_all.20), calls=%async_computation | async-start | bytes 8192 | tf_op jit(solution)/shard_map/all_to_all | solution.py:43
  23.7 72.4 %all-gather.3.cloned.1.call-start = ((), (), s32[]{:S(2)}) async-start(), calls=%async_computation.4 | async-start | bytes 3932160 | tf_op jit(solution)/shard_map/all_gather | solution.py:56
  29.6 56.2 %all-to-all-start.1 = ((bf16[8,72,2048]{2,1,0:T(8,128)(2,1)}), bf16[8,72,2048]{2,1,0:T(8,128)(2,1)S(1)}, u32[]{:S(2)}, u32[]{:S(2)}) async-start(bf16[8,72,2048]{2,1,0:T(8,128)(2,1)} %broadcast_select_fusion), calls=%async_computation.1 | async-start | bytes 4718592 | tf_op jit(solution)/shard_map/all_to_all | solution.py:36
  34.7 107.0 %reduce-scatter.4.cloned.1.call-start = ((), (), s32[]{:S(2)}) async-start(), calls=%async_computation.5 | async-start | bytes 3932160
  101.9 10.6 %all-to-all-start.2 = ((f32[8,1,72]{2,1,0:T(1,128)}), f32[8,1,72]{2,1,0:T(1,128)S(1)}, u32[]{:S(2)}, u32[]{:S(2)}) async-start(f32[8,1,72]{2,1,0:T(1,128)} %all_to_all.18), calls=%async_computation.2 | async-start | bytes 8192 | tf_op jit(solution)/shard_map/all_to_all | solution.py:68
Sparse Core Ops, SparseCore 0:
  26.3 44.5 all-gather.2
  96.2 45.4 reduce-scatter.3

commit v2 on v0

v2 whole, which is shorter than its diff:
```python
import functools

import jax
import jax.numpy as jnp
from jax import lax
from jax.experimental import pallas as pl
from jax.experimental.pallas import tpu as pltpu
from jax.sharding import PartitionSpec as P

MESH = pl.DeviceIdType.MESH
F32 = jnp.float32
BF16 = jnp.bfloat16
LANES = 128


def kernel(
    n_dp, n_ex, chunks,
    grad_ref, routes_ref, weights_ref, hidden_ref, shard_ref,
    hgrad_ref, wgrad_ref, rgrad_ref,
    pick, send, recv, full, scale_out, scale_in, term_out, term_in,
    hid, unscaled, part, landed,
    row_s, row_r, mat_s, mat_r, sca_s, sca_r, ter_s, ter_r, red_s, red_r,
):
    dp, ex = lax.axis_index("dp"), lax.axis_index("expert")
    cap = hidden_ref.shape[1]
    wide = send.shape[2]
    fc = send.shape[3]
    depth = shard_ref.shape[0]
    tokens = grad_ref.shape[0]
    ff = hidden_ref.shape[2]

    def columns(c):
        return pl.ds(pl.multiple_of(c * fc, fc), fc)

    def mat_copy(c, k):
        to = lax.rem(dp + k, n_dp)
        return pltpu.make_async_remote_copy(
            src_ref=shard_ref.at[:, columns(c)], dst_ref=full.at[c, dp],
            send_sem=mat_s.at[c, to], recv_sem=mat_r.at[c, dp],
            device_id=(to, ex), device_id_type=MESH)

    def mat_arrival(c, k):
        src = lax.rem(dp + k, n_dp)
        return pltpu.make_async_remote_copy(
            src_ref=shard_ref.at[:, columns(c)], dst_ref=full.at[c, src],
            send_sem=mat_s.at[c, src], recv_sem=mat_r.at[c, src],
            device_id=(src, ex), device_id_type=MESH)

    def row_copy(c, k):
        to = lax.rem(ex + k, n_ex)
        return pltpu.make_async_remote_copy(
            src_ref=send.at[c, to], dst_ref=recv.at[c, ex],
            send_sem=row_s.at[c, to], recv_sem=row_r.at[c, ex],
            device_id=(dp, to), device_id_type=MESH)

    def row_arrival(c, k):
        src = lax.rem(ex + k, n_ex)
        return pltpu.make_async_remote_copy(
            src_ref=send.at[c, src], dst_ref=recv.at[c, src],
            send_sem=row_s.at[c, src], recv_sem=row_r.at[c, src],
            device_id=(dp, src), device_id_type=MESH)

    def red_copy(c, k):
        to = lax.rem(dp + k, n_dp)
        return pltpu.make_async_remote_copy(
            src_ref=part.at[c, to], dst_ref=landed.at[c, dp],
            send_sem=red_s.at[c, to], recv_sem=red_r.at[c, dp],
            device_id=(to, ex), device_id_type=MESH)

    def red_arrival(c, k):
        src = lax.rem(dp + k, n_dp)
        return pltpu.make_async_remote_copy(
            src_ref=part.at[c, src], dst_ref=landed.at[c, src],
            send_sem=red_s.at[c, src], recv_sem=red_r.at[c, src],
            device_id=(src, ex), device_id_type=MESH)

    def small_copy(out, into, s, r, k):
        to = lax.rem(ex + k, n_ex)
        return pltpu.make_async_remote_copy(
            src_ref=out.at[to], dst_ref=into.at[ex],
            send_sem=s.at[to], recv_sem=r.at[ex],
            device_id=(dp, to), device_id_type=MESH)

    def small_arrival(out, into, s, r, k):
        src = lax.rem(ex + k, n_ex)
        return pltpu.make_async_remote_copy(
            src_ref=out.at[src], dst_ref=into.at[src],
            send_sem=s.at[src], recv_sem=r.at[src],
            device_id=(dp, src), device_id_type=MESH)

    def each(low, high, body):
        def step(i, carry):
            body(i)
            return carry
        lax.fori_loop(low, high, step, 0)

    barrier = pltpu.get_barrier_semaphore()
    each(1, n_dp, lambda k: pl.semaphore_signal(
        barrier, inc=1, device_id=(lax.rem(dp + k, n_dp), ex), device_id_type=MESH))
    each(1, n_ex, lambda k: pl.semaphore_signal(
        barrier, inc=1, device_id=(dp, lax.rem(ex + k, n_ex)), device_id_type=MESH))

    first, second = routes_ref[0:1, :], routes_ref[1:2, :]
    names = lax.broadcasted_iota(jnp.int32, (n_ex, tokens), 0)
    named = (names == first) | (names == second)
    earlier = (lax.broadcasted_iota(jnp.int32, (tokens, tokens), 0)
               < lax.broadcasted_iota(jnp.int32, (tokens, tokens), 1))
    rank = jnp.dot(jnp.where(named, 1.0, 0.0).astype(BF16),
                   jnp.where(earlier, 1.0, 0.0).astype(BF16), preferred_element_type=F32)
    rank = jnp.where(named, rank.astype(jnp.int32), -1)
    scale_of = (jnp.where(names == first, weights_ref[0:1, :], 0.0)
                + jnp.where(names == second, weights_ref[1:2, :], 0.0))
    place = lax.broadcasted_iota(jnp.int32, (wide, tokens), 0)
    diagonal = (lax.broadcasted_iota(jnp.int32, (wide, LANES), 0)
                == lax.broadcasted_iota(jnp.int32, (wide, LANES), 1))
    for e in range(n_ex):
        chosen = place == rank[e:e + 1, :]
        pick[e * wide:(e + 1) * wide, :] = jnp.where(chosen, 1.0, 0.0).astype(BF16)
        column = jnp.sum(jnp.where(chosen, scale_of[e:e + 1, :], 0.0), axis=1, keepdims=True)
        row = jnp.sum(jnp.where(diagonal, column, 0.0), axis=0, keepdims=True)
        scale_out[e] = jnp.broadcast_to(row, (8, LANES))

    pl.semaphore_wait(barrier, n_dp + n_ex - 2)
    each(1, n_ex, lambda k: small_copy(scale_out, scale_in, sca_s, sca_r, k).start())
    scale_in[ex] = scale_out[ex]

    def dispatch(c):
        rows = jnp.dot(pick[...], grad_ref[:, columns(c)], preferred_element_type=F32)
        send[c] = rows.astype(BF16).reshape(n_ex, wide, fc)
        each(1, n_ex, lambda k: row_copy(c, k).start())
        each(1, n_dp, lambda k: mat_copy(c, k).start())
        recv[c, ex] = send[c, ex]
        full[c, dp] = shard_ref[:, columns(c)]
    each(0, chunks, dispatch)

    padded = jnp.concatenate(
        [hidden_ref[...].astype(F32), jnp.zeros((n_ex, wide - cap, ff), F32)], axis=1)
    hid[...] = padded.reshape(n_ex * wide, ff).T.astype(BF16)

    each(1, n_ex, lambda k: small_arrival(scale_out, scale_in, sca_s, sca_r, k).wait())

    def scale_column():
        return jnp.concatenate(
            [jnp.sum(jnp.where(diagonal, scale_in[j, 0:1, :], 0.0), axis=1, keepdims=True)
             for j in range(n_ex)], axis=0)

    def work(c):
        each(1, n_ex, lambda k: row_arrival(c, k).wait())
        rows = recv[c].reshape(n_ex * wide, fc)
        weighted = (scale_column() * rows.astype(F32)).astype(BF16)
        share = jnp.dot(hid[...], weighted, preferred_element_type=F32)
        part[c] = share.astype(BF16).reshape(n_dp, depth, fc)
        each(1, n_dp, lambda k: red_copy(c, k).start())
        landed[c, dp] = part[c, dp]
        each(1, n_dp, lambda k: mat_arrival(c, k).wait())
        product = lax.dot_general(
            rows, full[c].reshape(n_dp * depth, fc), (((1,), (1,)), ((), ())),
            preferred_element_type=F32)

        @pl.when(c == 0)
        def _():
            unscaled[...] = product

        @pl.when(c > 0)
        def _():
            unscaled[...] += product
    each(0, chunks, work)

    for j in range(n_ex):
        block = unscaled[j * wide:j * wide + cap, :]
        term = jnp.sum(hidden_ref[j].astype(F32) * block, axis=1, keepdims=True)
        row = jnp.sum(jnp.where(diagonal[0:cap], term, 0.0), axis=0, keepdims=True)
        term_out[j] = jnp.broadcast_to(row, (8, LANES))
    each(1, n_ex, lambda k: small_copy(term_out, term_in, ter_s, ter_r, k).start())
    term_in[ex] = term_out[ex]
    for j in range(n_ex):
        column = jnp.sum(jnp.where(diagonal, scale_in[j, 0:1, :], 0.0), axis=1, keepdims=True)
        hgrad_ref[j] = (column[0:cap] * unscaled[j * wide:j * wide + cap, :]).astype(BF16)

    def reduce(c):
        each(1, n_dp, lambda k: red_arrival(c, k).wait())
        wgrad_ref[:, columns(c)] = jnp.sum(landed[c].astype(F32), axis=0)
    each(0, chunks, reduce)

    each(1, n_ex, lambda k: small_arrival(term_out, term_in, ter_s, ter_r, k).wait())
    first_out = jnp.zeros((1, tokens), F32)
    second_out = jnp.zeros((1, tokens), F32)
    for e in range(n_ex):
        column = jnp.sum(jnp.where(diagonal, term_in[e, 0:1, :], 0.0), axis=1, keepdims=True)
        back = jnp.sum(jnp.where(place == rank[e:e + 1, :], column, 0.0), axis=0, keepdims=True)
        first_out += jnp.where(first == e, back, 0.0)
        second_out += jnp.where(second == e, back, 0.0)
    rgrad_ref[0:1, :] = first_out
    rgrad_ref[1:2, :] = second_out


def per_device(output_grad, routes, combine_weights, saved_hidden, down_weight):
    n_dp, n_ex = lax.axis_size("dp"), lax.axis_size("expert")
    tokens, features = output_grad.shape
    slots, ff = saved_hidden.shape
    cap = slots // n_ex
    wide = -(-cap // 16) * 16
    depth = down_weight.shape[1]
    chunks = 4
    fc = features // chunks
    dma = pltpu.SemaphoreType.DMA
    hgrad, wgrad, rgrad = pl.pallas_call(
        functools.partial(kernel, n_dp, n_ex, chunks),
        out_shape=(
            jax.ShapeDtypeStruct((n_ex, cap, ff), BF16),
            jax.ShapeDtypeStruct((depth, features), F32),
            jax.ShapeDtypeStruct((2, tokens), F32),
        ),
        in_specs=[pl.BlockSpec(memory_space=pltpu.VMEM)] * 5,
        out_specs=[pl.BlockSpec(memory_space=pltpu.VMEM)] * 3,
        scratch_shapes=[
            pltpu.VMEM((n_ex * wide, tokens), BF16),
            pltpu.VMEM((chunks, n_ex, wide, fc), BF16),
            pltpu.VMEM((chunks, n_ex, wide, fc), BF16),
            pltpu.VMEM((chunks, n_dp, depth, fc), BF16),
            pltpu.VMEM((n_ex, 8, LANES), F32),
            pltpu.VMEM((n_ex, 8, LANES), F32),
            pltpu.VMEM((n_ex, 8, LANES), F32),
            pltpu.VMEM((n_ex, 8, LANES), F32),
            pltpu.VMEM((ff, n_ex * wide), BF16),
            pltpu.VMEM((n_ex * wide, ff), F32),
            pltpu.VMEM((chunks, n_dp, depth, fc), BF16),
            pltpu.VMEM((chunks, n_dp, depth, fc), BF16),
            dma((chunks, n_ex)), dma((chunks, n_ex)),
            dma((chunks, n_dp)), dma((chunks, n_dp)),
            dma((n_ex,)), dma((n_ex,)), dma((n_ex,)), dma((n_ex,)),
            dma((chunks, n_dp)), dma((chunks, n_dp)),
        ],
        compiler_params=pltpu.CompilerParams(
            collective_id=0, has_side_effects=True, vmem_limit_bytes=52 * 2**20
        ),
        cost_estimate=pl.CostEstimate(
            flops=4 * slots * features * ff, bytes_accessed=8 * 2**20, transcendentals=0),
    )(
        output_grad, routes.T, combine_weights.T.astype(F32),
        saved_hidden.reshape(n_ex, cap, ff), down_weight[0],
    )
    return hgrad.reshape(slots, ff), wgrad[None], rgrad.T


def solution(mesh):
    return jax.shard_map(
        per_device,
        mesh=mesh,
        in_specs=(
            P(("dp", "expert"), None),
            P(("dp", "expert"), None),
            P(("dp", "expert"), None),
            P(("dp", "expert"), None),
            P("expert", "dp", None),
        ),
        out_specs=(P(("dp", "expert"), None), P("expert", "dp", None), P(("dp", "expert"), None)),
        check_vma=False,
    )
```

time: 157 us -> 88.5 us (0.56)
  waiting for transfers between devices: 80.9 us -> 0 us
  Pallas kernels: 0 us -> 79.3 us
  local copies, waits for them, and re-layouts: 26.3 us -> 6.92 us
  starting transfers between devices: 17.5 us -> 0 us
  between operations: 14.2 us -> 0.65 us
  matrix products: 10.6 us -> 0 us
  other arithmetic: 5.47 us -> 0.68 us
    pallas_call x0 -> x1, Pallas kernels: none -> 79.3 us  [per_device(): pl.pallas_call(functools.partial(kernel, n_dp, n_ex, chunks), out_shape=(...]
    all_to_all x3 -> x0, waiting for transfers between devices: 54.8 us -> none  [the longest x1 51 us: per_device(): lax.all_to_all(send_rows.reshape(experts, capacity, features), 'expert',...]
    unnamed x3 -> x0, waiting for transfers between devices: 26 us -> none
    all_to_all x3 -> x0, starting transfers between devices: 17.5 us -> none  [the longest x1 6.78 us: per_device(): lax.all_to_all(route_terms.reshape(experts, capacity), 'expert', split_ax...]
    dot_general x2 -> x0, matrix products: 10.6 us -> none  [the longest x1 5.53 us: per_device(): lax.dot_general(saved_hidden, weighted, (((0,), (0,)), ((), ())), preferr...]
    gather x3 -> x0, local copies, waits for them, and re-layouts: 9.23 us -> none  [the longest x1 3.95 us: per_device(): combine_weights.reshape(-1)[safe_index]]
    unnamed x8 -> x11, local copies, waits for them, and re-layouts: 11 us -> 6.92 us
    scatter x1 -> x0, local copies, waits for them, and re-layouts: 2.92 us -> none  [per_device(): source = jnp.full((slot_count,), route_total, jnp.int32).at[target].set(j...]
  transfers between devices with their start and end apart: 5 -> 0, of which waited for: 3 -> 0; matrix products, arithmetic and copies ran while one was open for 16% -> 0% of each run, Pallas kernels for 0% -> 0%
where the time goes in v2:
time: 88.5 us; the launch traced here: 87.6 us
  Pallas kernels  79.3 us (90%)
  local copies, waits for them, and re-layouts  6.92 us (8%)
    pallas_call x1, Pallas kernels, per_device(): pl.pallas_call(functools.partial(kernel, n_dp, n_ex, chunks), out_shape=(...  79.3 us
    unnamed x11, local copies, waits for them, and re-layouts  6.92 us

profile of v2, /device:TPU:11, one launch (start us, length us, event | category | flops | bytes accessed | tf_op | source)
XLA Modules:
  0.0 87.6 jit_solution(16115299213465705965)
XLA Ops:
  0.6 0.7 convert_bitcast_fusion.weights_ref
  1.3 0.0 copy-start
  1.3 1.1 %copy-done = bf16[192,2048]{1,0:T(8,128)(2,1)S(1)} copy-done((bf16[192,2048]{1,0:T(8,128)(2,1)S(1)}, bf16[192,2048]{1,0:T(8,128)(2,1)}, u32[]{:S(2)}) %copy-start) | copy-done | bytes 786456
  2.4 0.0 copy-start.1
  2.4 1.1 %copy-done.1 = bf16[1,192,2048]{2,1,0:T(8,128)(2,1)S(1)} copy-done((bf16[1,192,2048]{2,1,0:T(8,128)(2,1)S(1)}, bf16[1,192,2048]{2,1,0:T(8,128)(2,1)}, u32[]{:S(2)}) %copy-start.1) | copy-done | bytes 786456
  3.6 0.0 copy-start.2
  3.6 0.7 copy-done.2
  4.3 79.3 %shard_map.76 = (bf16[8,72,768]{2,1,0:T(8,128)(2,1)}, f32[192,2048]{1,0:T(8,128)}, f32[2,192]{1,0:T(2,128)S(1)}) custom-call(bf16[192,2048]{1,0:T(8,128)(2,1)S(1)} %copy-done, s32[2,192]{1,0:T(2,128)S(1)} %bitcast.10, f32[2,192]{1,0:T(2,128)S(1)} %convert_bitcast_fusion.weights_ref, bf16[8,72,768]{2,1,0:T(8,128)(2,1)} %bitcast.13, bf16[192,2048]{1,0:T(8,128)(2,1)S(1)} %bitcast.9), custom_call_target="tpu_custom_call" | custom-call | flops 3623878656 | bytes 8388608 | tf_op jit(solution)/shard_map/pallas_call | solution.py:207
  83.6 0.0 copy-start.3
  83.6 2.3 %copy.11 = bf16[576,768]{1,0:T(8,128)(2,1)} copy(bf16[576,768]{1,0:T(8,128)(2,1)} %bitcast.12) | data formatting | bytes 1769472
  85.8 0.0 copy-done.3
  85.8 1.1 %copy.12 = f32[1,192,2048]{2,1,0:T(8,128)} copy(f32[1,192,2048]{2,1,0:T(8,128)S(1)} %bitcast.11) | data formatting | bytes 3145728
  87.0 0.6 copy.13
Async XLA Ops:
  1.3 1.1 %copy-start = (bf16[192,2048]{1,0:T(8,128)(2,1)S(1)}, bf16[192,2048]{1,0:T(8,128)(2,1)}, u32[]{:S(2)}) copy-start(bf16[192,2048]{1,0:T(8,128)(2,1)} %grad_ref.1) | copy-start | bytes 2359300
  2.4 1.1 %copy-start.1 = (bf16[1,192,2048]{2,1,0:T(8,128)(2,1)S(1)}, bf16[1,192,2048]{2,1,0:T(8,128)(2,1)}, u32[]{:S(2)}) copy-start(bf16[1,192,2048]{2,1,0:T(8,128)(2,1)} %param.9) | copy-start | bytes 2359300
  3.6 0.7 copy-start.2
  83.6 2.3 %copy-start.3 = (f32[192,2048]{1,0:T(8,128)S(1)}, f32[192,2048]{1,0:T(8,128)}, u32[]{:S(2)}) copy-start(f32[192,2048]{1,0:T(8,128)} %get-tuple-element.7) | copy-start | bytes 4718596

commit v3 on v2

--- a/solution.py
+++ b/solution.py
@@ -23,8 +23,9 @@
 ):
     dp, ex = lax.axis_index("dp"), lax.axis_index("expert")
     cap = hidden_ref.shape[1]
-    wide = send.shape[2]
-    fc = send.shape[3]
+    wide = send.shape[2] // 2
+    sub = send.shape[3]
+    fc = 2 * sub
     depth = shard_ref.shape[0]
     tokens = grad_ref.shape[0]
     ff = hidden_ref.shape[2]
@@ -32,19 +33,84 @@
     def columns(c):
         return pl.ds(pl.multiple_of(c * fc, fc), fc)
 
-    def mat_copy(c, k):
+    def dp_copy(src, dst, s, r, to):
+        return pltpu.make_async_remote_copy(
+            src_ref=src, dst_ref=dst, send_sem=s, recv_sem=r,
+            device_id=(to, ex), device_id_type=MESH)
+
+    def narrow(t):
+        return pl.ds(pl.multiple_of(t * sub, sub), sub)
+
+    square = n_dp == 4
+    across = dp + 1 - 2 * lax.rem(dp, 2)
+    along = lax.rem(dp + 2, n_dp)
+    corner = lax.rem(across + 2, n_dp)
+    near = (across, along)
+
+    def mat_copy(t, to):
+        return dp_copy(shard_ref.at[:, narrow(t)], full.at[t, dp], mat_s.at[t, to], mat_r.at[t, dp], to)
+
+    def mat_pass(t, h):
+        return dp_copy(full.at[t, near[h]], full.at[t, near[h]], mat_s.at[t, corner],
+                       mat_r.at[t, near[h]], near[1 - h])
+
+    def mat_arrival(t, src):
+        return dp_copy(shard_ref.at[:, narrow(t)], full.at[t, src], mat_s.at[t, src], mat_r.at[t, src], src)
+
+    def mat_start(t):
+        if square:
+            mat_copy(t, across).start()
+            mat_copy(t, along).start()
+        else:
+            each(1, n_dp, lambda k: mat_copy(t, lax.rem(dp + k, n_dp)).start())
+
+    def mat_forward(t, h):
+        if square:
+            mat_arrival(t, near[h]).wait_recv()
+            mat_pass(t, h).start()
+
+    def mat_wait(t, h):
+        if square:
+            mat_arrival(t, near[1 - h]).wait_recv()
+            mat_arrival(t, corner).wait()
+            mat_arrival(t, across).wait_send()
+            mat_arrival(t, along).wait_send()
+        else:
+            each(1, n_dp, lambda k: mat_arrival(t, lax.rem(dp + k, n_dp)).wait())
+
+    def red_copy(t, block, slot, to):
+        return dp_copy(part.at[t, block], landed.at[t, slot], red_s.at[t, slot], red_r.at[t, slot], to)
+
+    def red_far(t, k):
         to = lax.rem(dp + k, n_dp)
-        return pltpu.make_async_remote_copy(
-            src_ref=shard_ref.at[:, columns(c)], dst_ref=full.at[c, dp],
-            send_sem=mat_s.at[c, to], recv_sem=mat_r.at[c, dp],
-            device_id=(to, ex), device_id_type=MESH)
-
-    def mat_arrival(c, k):
+        return dp_copy(part.at[t, to], landed.at[t, dp], red_s.at[t, to], red_r.at[t, dp], to)
+
+    def red_far_arrival(t, k):
         src = lax.rem(dp + k, n_dp)
-        return pltpu.make_async_remote_copy(
-            src_ref=shard_ref.at[:, columns(c)], dst_ref=full.at[c, src],
-            send_sem=mat_s.at[c, src], recv_sem=mat_r.at[c, src],
-            device_id=(src, ex), device_id_type=MESH)
+        return dp_copy(part.at[t, src], landed.at[t, src], red_s.at[t, src], red_r.at[t, src], src)
+
+    def red_start(t, h):
+        if square:
+            red_copy(t, corner, 1, near[h]).start()
+            red_copy(t, near[h], 0, near[h]).start()
+        else:
+            each(1, n_dp, lambda k: red_far(t, k).start())
+
+    def red_forward(t, h):
+        if square:
+            red_copy(t, corner, 1, near[h]).wait()
+            total = part[t, near[1 - h]].astype(F32) + landed[t, 1].astype(F32)
+            part[t, near[1 - h]] = total.astype(BF16)
+            red_copy(t, near[1 - h], 2, near[1 - h]).start()
+
+    def red_finish(t, h):
+        if square:
+            red_copy(t, near[h], 0, near[h]).wait()
+            red_copy(t, near[1 - h], 2, near[1 - h]).wait()
+            return part[t, dp].astype(F32) + landed[t, 0].astype(F32) + landed[t, 2].astype(F32)
+        each(1, n_dp, lambda k: red_far_arrival(t, k).wait())
+        landed[t, dp] = part[t, dp]
+        return jnp.sum(landed[t].astype(F32), axis=0)
 
     def row_copy(c, k):
         to = lax.rem(ex + k, n_ex)
@@ -59,20 +125,6 @@
             src_ref=send.at[c, src], dst_ref=recv.at[c, src],
             send_sem=row_s.at[c, src], recv_sem=row_r.at[c, src],
             device_id=(dp, src), device_id_type=MESH)
-
-    def red_copy(c, k):
-        to = lax.rem(dp + k, n_dp)
-        return pltpu.make_async_remote_copy(
-            src_ref=part.at[c, to], dst_ref=landed.at[c, dp],
-            send_sem=red_s.at[c, to], recv_sem=red_r.at[c, dp],
-            device_id=(to, ex), device_id_type=MESH)
-
-    def red_arrival(c, k):
-        src = lax.rem(dp + k, n_dp)
-        return pltpu.make_async_remote_copy(
-            src_ref=part.at[c, src], dst_ref=landed.at[c, src],
-            send_sem=red_s.at[c, src], recv_sem=red_r.at[c, src],
-            device_id=(src, ex), device_id_type=MESH)
 
     def small_copy(out, into, s, r, k):
         to = lax.rem(ex + k, n_ex)
@@ -113,28 +165,34 @@
     place = lax.broadcasted_iota(jnp.int32, (wide, tokens), 0)
     diagonal = (lax.broadcasted_iota(jnp.int32, (wide, LANES), 0)
                 == lax.broadcasted_iota(jnp.int32, (wide, LANES), 1))
+    picked = []
     for e in range(n_ex):
         chosen = place == rank[e:e + 1, :]
-        pick[e * wide:(e + 1) * wide, :] = jnp.where(chosen, 1.0, 0.0).astype(BF16)
+        picked.append(jnp.where(chosen, 1.0, 0.0))
         column = jnp.sum(jnp.where(chosen, scale_of[e:e + 1, :], 0.0), axis=1, keepdims=True)
         row = jnp.sum(jnp.where(diagonal, column, 0.0), axis=0, keepdims=True)
         scale_out[e] = jnp.broadcast_to(row, (8, LANES))
 
+    pick[...] = jnp.concatenate(picked, axis=0).astype(BF16)
     pl.semaphore_wait(barrier, n_dp + n_ex - 2)
     each(1, n_ex, lambda k: small_copy(scale_out, scale_in, sca_s, sca_r, k).start())
     scale_in[ex] = scale_out[ex]
 
     def dispatch(c):
         rows = jnp.dot(pick[...], grad_ref[:, columns(c)], preferred_element_type=F32)
-        send[c] = rows.astype(BF16).reshape(n_ex, wide, fc)
+        send[c] = jnp.concatenate(
+            [rows[:, :sub].reshape(n_ex, wide, sub), rows[:, sub:].reshape(n_ex, wide, sub)],
+            axis=1).astype(BF16)
         each(1, n_ex, lambda k: row_copy(c, k).start())
-        each(1, n_dp, lambda k: mat_copy(c, k).start())
         recv[c, ex] = send[c, ex]
-        full[c, dp] = shard_ref[:, columns(c)]
+        for h in range(2):
+            mat_start(2 * c + h)
+            full[2 * c + h, dp] = shard_ref[:, narrow(2 * c + h)]
     each(0, chunks, dispatch)
 
-    padded = jnp.concatenate(
-        [hidden_ref[...].astype(F32), jnp.zeros((n_ex, wide - cap, ff), F32)], axis=1)
+    padded = hidden_ref[...].astype(F32)
+    if wide > cap:
+        padded = jnp.concatenate([padded, jnp.zeros((n_ex, wide - cap, ff), F32)], axis=1)
     hid[...] = padded.reshape(n_ex * wide, ff).T.astype(BF16)
 
     each(1, n_ex, lambda k: small_arrival(scale_out, scale_in, sca_s, sca_r, k).wait())
@@ -144,18 +202,26 @@
             [jnp.sum(jnp.where(diagonal, scale_in[j, 0:1, :], 0.0), axis=1, keepdims=True)
              for j in range(n_ex)], axis=0)
 
+    def pass_on(c):
+        for h in range(2):
+            mat_forward(2 * c + h, h)
+    each(0, chunks, pass_on)
+
     def work(c):
         each(1, n_ex, lambda k: row_arrival(c, k).wait())
-        rows = recv[c].reshape(n_ex * wide, fc)
-        weighted = (scale_column() * rows.astype(F32)).astype(BF16)
-        share = jnp.dot(hid[...], weighted, preferred_element_type=F32)
-        part[c] = share.astype(BF16).reshape(n_dp, depth, fc)
-        each(1, n_dp, lambda k: red_copy(c, k).start())
-        landed[c, dp] = part[c, dp]
-        each(1, n_dp, lambda k: mat_arrival(c, k).wait())
-        product = lax.dot_general(
-            rows, full[c].reshape(n_dp * depth, fc), (((1,), (1,)), ((), ())),
-            preferred_element_type=F32)
+        both = recv[c].astype(F32)
+        halves = [both[:, h * wide:(h + 1) * wide].reshape(n_ex * wide, sub) for h in range(2)]
+        for h in range(2):
+            weighted = (scale_column() * halves[h]).astype(BF16)
+            share = jnp.dot(hid[...], weighted, preferred_element_type=F32)
+            part[2 * c + h] = share.astype(BF16).reshape(n_dp, depth, sub)
+            red_start(2 * c + h, h)
+        product = jnp.zeros(unscaled.shape, F32)
+        for h in range(2):
+            mat_wait(2 * c + h, h)
+            product += lax.dot_general(
+                halves[h].astype(BF16), full[2 * c + h].reshape(n_dp * depth, sub),
+                (((1,), (1,)), ((), ())), preferred_element_type=F32)
 
         @pl.when(c == 0)
         def _():
@@ -164,6 +230,8 @@
         @pl.when(c > 0)
         def _():
             unscaled[...] += product
+            for h in range(2):
+                red_forward(2 * (c - 1) + h, h)
     each(0, chunks, work)
 
     for j in range(n_ex):
@@ -177,9 +245,12 @@
         column = jnp.sum(jnp.where(diagonal, scale_in[j, 0:1, :], 0.0), axis=1, keepdims=True)
         hgrad_ref[j] = (column[0:cap] * unscaled[j * wide:j * wide + cap, :]).astype(BF16)
 
+    for h in range(2):
+        red_forward(2 * (chunks - 1) + h, h)
+
     def reduce(c):
-        each(1, n_dp, lambda k: red_arrival(c, k).wait())
-        wgrad_ref[:, columns(c)] = jnp.sum(landed[c].astype(F32), axis=0)
+        for h in range(2):
+            wgrad_ref[:, narrow(2 * c + h)] = red_finish(2 * c + h, h)
     each(0, chunks, reduce)
 
     each(1, n_ex, lambda k: small_arrival(term_out, term_in, ter_s, ter_r, k).wait())
@@ -199,10 +270,10 @@
     tokens, features = output_grad.shape
     slots, ff = saved_hidden.shape
     cap = slots // n_ex
-    wide = -(-cap // 16) * 16
+    wide = -(-cap // 8) * 8
     depth = down_weight.shape[1]
     chunks = 4
-    fc = features // chunks
+    sub = features // (2 * chunks)
     dma = pltpu.SemaphoreType.DMA
     hgrad, wgrad, rgrad = pl.pallas_call(
         functools.partial(kernel, n_dp, n_ex, chunks),
@@ -215,24 +286,24 @@
         out_specs=[pl.BlockSpec(memory_space=pltpu.VMEM)] * 3,
         scratch_shapes=[
             pltpu.VMEM((n_ex * wide, tokens), BF16),
-            pltpu.VMEM((chunks, n_ex, wide, fc), BF16),
-            pltpu.VMEM((chunks, n_ex, wide, fc), BF16),
-            pltpu.VMEM((chunks, n_dp, depth, fc), BF16),
+            pltpu.VMEM((chunks, n_ex, 2 * wide, sub), BF16),
+            pltpu.VMEM((chunks, n_ex, 2 * wide, sub), BF16),
+            pltpu.VMEM((2 * chunks, n_dp, depth, sub), BF16),
             pltpu.VMEM((n_ex, 8, LANES), F32),
             pltpu.VMEM((n_ex, 8, LANES), F32),
             pltpu.VMEM((n_ex, 8, LANES), F32),
             pltpu.VMEM((n_ex, 8, LANES), F32),
             pltpu.VMEM((ff, n_ex * wide), BF16),
             pltpu.VMEM((n_ex * wide, ff), F32),
-            pltpu.VMEM((chunks, n_dp, depth, fc), BF16),
-            pltpu.VMEM((chunks, n_dp, depth, fc), BF16),
+            pltpu.VMEM((2 * chunks, n_dp, depth, sub), BF16),
+            pltpu.VMEM((2 * chunks, n_dp, depth, sub), BF16),
             dma((chunks, n_ex)), dma((chunks, n_ex)),
-            dma((chunks, n_dp)), dma((chunks, n_dp)),
+            dma((2 * chunks, n_dp)), dma((2 * chunks, n_dp)),
             dma((n_ex,)), dma((n_ex,)), dma((n_ex,)), dma((n_ex,)),
-            dma((chunks, n_dp)), dma((chunks, n_dp)),
+            dma((2 * chunks, n_dp)), dma((2 * chunks, n_dp)),
         ],
         compiler_params=pltpu.CompilerParams(
-            collective_id=0, has_side_effects=True, vmem_limit_bytes=52 * 2**20
+            collective_id=0, has_side_effects=True, vmem_limit_bytes=36 * 2**20
         ),
         cost_estimate=pl.CostEstimate(
             flops=4 * slots * features * ff, bytes_accessed=8 * 2**20, transcendentals=0),

time: 88.5 us -> 79.1 us (0.89)
  Pallas kernels: 79.3 us -> 70.8 us
    pallas_call x1, Pallas kernels: 79.3 us -> 70.8 us  [per_device(): pl.pallas_call(functools.partial(kernel, n_dp, n_ex, chunks), out_shape=(...]
where the time goes in v3:
time: 79.1 us; the launch traced here: 78.9 us
  Pallas kernels  70.8 us (90%)
  local copies, waits for them, and re-layouts  6.75 us (9%)
    pallas_call x1, Pallas kernels, per_device(): pl.pallas_call(functools.partial(kernel, n_dp, n_ex, chunks), out_shape=(...  70.8 us
    unnamed x11, local copies, waits for them, and re-layouts  6.75 us

profile of v3, /device:TPU:11, one launch (start us, length us, event | category | flops | bytes accessed | tf_op | source)
XLA Modules:
  0.0 78.9 jit_solution(1041678671115738833)
XLA Ops:
  0.6 0.7 convert_bitcast_fusion.weights_ref
  1.3 0.0 copy-start
  1.3 1.2 %copy-done = bf16[576,768]{1,0:T(8,128)(2,1)S(1)} copy-done((bf16[576,768]{1,0:T(8,128)(2,1)S(1)}, bf16[576,768]{1,0:T(8,128)(2,1)}, u32[]{:S(2)}) %copy-start) | copy-done | bytes 884760
  2.5 0.0 copy-start.1
  2.5 1.1 %copy-done.1 = bf16[192,2048]{1,0:T(8,128)(2,1)S(1)} copy-done((bf16[192,2048]{1,0:T(8,128)(2,1)S(1)}, bf16[192,2048]{1,0:T(8,128)(2,1)}, u32[]{:S(2)}) %copy-start.1) | copy-done | bytes 786456
  3.6 0.0 copy-start.2
  3.6 1.1 %copy-done.2 = bf16[1,192,2048]{2,1,0:T(8,128)(2,1)S(1)} copy-done((bf16[1,192,2048]{2,1,0:T(8,128)(2,1)S(1)}, bf16[1,192,2048]{2,1,0:T(8,128)(2,1)}, u32[]{:S(2)}) %copy-start.2) | copy-done | bytes 786456
  4.7 0.0 copy-start.3
  4.7 0.7 copy-done.3
  5.4 70.8 %shard_map.76 = (bf16[8,72,768]{2,1,0:T(8,128)(2,1)S(1)}, f32[192,2048]{1,0:T(8,128)S(1)}, f32[2,192]{1,0:T(2,128)S(1)}) custom-call(bf16[192,2048]{1,0:T(8,128)(2,1)S(1)} %copy-done.1, s32[2,192]{1,0:T(2,128)S(1)} %bitcast.13, f32[2,192]{1,0:T(2,128)S(1)} %convert_bitcast_fusion.weights_ref, bf16[8,72,768]{2,1,0:T(8,128)(2,1)S(1)} %bitcast.11, ...), custom_call_target="tpu_custom_call" | custom-call | flops 3623878656 | bytes 8388608 | tf_op jit(solution)/shard_map/pallas_call | solution.py:278
  76.2 0.9 %copy.11 = bf16[576,768]{1,0:T(8,128)(2,1)} copy(bf16[576,768]{1,0:T(8,128)(2,1)S(1)} %bitcast.9) | data formatting | bytes 1769472
  77.1 1.1 %copy.12 = f32[1,192,2048]{2,1,0:T(8,128)} copy(f32[1,192,2048]{2,1,0:T(8,128)S(1)} %bitcast.8) | data formatting | bytes 3145728
  78.3 0.6 copy.13
Async XLA Ops:
  1.3 1.2 %copy-start = (bf16[576,768]{1,0:T(8,128)(2,1)S(1)}, bf16[576,768]{1,0:T(8,128)(2,1)}, u32[]{:S(2)}) copy-start(bf16[576,768]{1,0:T(8,128)(2,1)} %param.8) | copy-start | bytes 2654212
  2.5 1.1 %copy-start.1 = (bf16[192,2048]{1,0:T(8,128)(2,1)S(1)}, bf16[192,2048]{1,0:T(8,128)(2,1)}, u32[]{:S(2)}) copy-start(bf16[192,2048]{1,0:T(8,128)(2,1)} %grad_ref.1) | copy-start | bytes 2359300
  3.6 1.1 %copy-start.2 = (bf16[1,192,2048]{2,1,0:T(8,128)(2,1)S(1)}, bf16[1,192,2048]{2,1,0:T(8,128)(2,1)}, u32[]{:S(2)}) copy-start(bf16[1,192,2048]{2,1,0:T(8,128)(2,1)} %param.9) | copy-start | bytes 2359300
  4.7 0.7 copy-start.3

commit v4 on v3

--- a/solution.py
+++ b/solution.py
@@ -175,8 +175,6 @@
 
     pick[...] = jnp.concatenate(picked, axis=0).astype(BF16)
     pl.semaphore_wait(barrier, n_dp + n_ex - 2)
-    each(1, n_ex, lambda k: small_copy(scale_out, scale_in, sca_s, sca_r, k).start())
-    scale_in[ex] = scale_out[ex]
 
     def dispatch(c):
         rows = jnp.dot(pick[...], grad_ref[:, columns(c)], preferred_element_type=F32)
@@ -184,11 +182,20 @@
             [rows[:, :sub].reshape(n_ex, wide, sub), rows[:, sub:].reshape(n_ex, wide, sub)],
             axis=1).astype(BF16)
         each(1, n_ex, lambda k: row_copy(c, k).start())
+
+        @pl.when(c == 0)
+        def _():
+            each(1, n_ex, lambda k: small_copy(scale_out, scale_in, sca_s, sca_r, k).start())
+            scale_in[ex] = scale_out[ex]
+        for h in range(2):
+            mat_start(2 * c + h)
+    each(0, chunks, dispatch)
+
+    def keep_own(c):
         recv[c, ex] = send[c, ex]
         for h in range(2):
-            mat_start(2 * c + h)
             full[2 * c + h, dp] = shard_ref[:, narrow(2 * c + h)]
-    each(0, chunks, dispatch)
+    each(0, chunks, keep_own)
 
     padded = hidden_ref[...].astype(F32)
     if wide > cap:
@@ -207,12 +214,14 @@
             mat_forward(2 * c + h, h)
     each(0, chunks, pass_on)
 
+    scale = scale_column()
+
     def work(c):
         each(1, n_ex, lambda k: row_arrival(c, k).wait())
         both = recv[c].astype(F32)
         halves = [both[:, h * wide:(h + 1) * wide].reshape(n_ex * wide, sub) for h in range(2)]
         for h in range(2):
-            weighted = (scale_column() * halves[h]).astype(BF16)
+            weighted = (scale * halves[h]).astype(BF16)
             share = jnp.dot(hid[...], weighted, preferred_element_type=F32)
             part[2 * c + h] = share.astype(BF16).reshape(n_dp, depth, sub)
             red_start(2 * c + h, h)
@@ -241,12 +250,11 @@
         term_out[j] = jnp.broadcast_to(row, (8, LANES))
     each(1, n_ex, lambda k: small_copy(term_out, term_in, ter_s, ter_r, k).start())
     term_in[ex] = term_out[ex]
-    for j in range(n_ex):
-        column = jnp.sum(jnp.where(diagonal, scale_in[j, 0:1, :], 0.0), axis=1, keepdims=True)
-        hgrad_ref[j] = (column[0:cap] * unscaled[j * wide:j * wide + cap, :]).astype(BF16)
-
     for h in range(2):
         red_forward(2 * (chunks - 1) + h, h)
+
+    for j in range(n_ex):
+        hgrad_ref[j] = (scale[j * wide:j * wide + cap] * unscaled[j * wide:j * wide + cap, :]).astype(BF16)
 
     def reduce(c):
         for h in range(2):
@@ -272,7 +280,7 @@
     cap = slots // n_ex
     wide = -(-cap // 8) * 8
     depth = down_weight.shape[1]
-    chunks = 4
+    chunks = 8
     sub = features // (2 * chunks)
     dma = pltpu.SemaphoreType.DMA
     hgrad, wgrad, rgrad = pl.pallas_call(

time: 79.1 us -> 76.9 us (0.972); the launches traced: 78.9 us -> 75.7 us
  Pallas kernels: 70.8 us -> 67.7 us
    pallas_call x1, Pallas kernels: 70.8 us -> 67.7 us  [per_device(): pl.pallas_call(functools.partial(kernel, n_dp, n_ex, chunks), out_shape=(...]
where the time goes in v4:
time: 76.9 us; the launch traced here: 75.7 us
  Pallas kernels  67.7 us (88%)
  local copies, waits for them, and re-layouts  6.75 us (9%)
    pallas_call x1, Pallas kernels, per_device(): pl.pallas_call(functools.partial(kernel, n_dp, n_ex, chunks), out_shape=(...  67.7 us
    unnamed x11, local copies, waits for them, and re-layouts  6.75 us

profile of v4, /device:TPU:11, one launch (start us, length us, event | category | flops | bytes accessed | tf_op | source)
XLA Modules:
  0.0 75.7 jit_solution(15166410332085387310)
XLA Ops:
  0.6 0.7 convert_bitcast_fusion.weights_ref
  1.3 0.0 copy-start
  1.3 1.2 %copy-done = bf16[576,768]{1,0:T(8,128)(2,1)S(1)} copy-done((bf16[576,768]{1,0:T(8,128)(2,1)S(1)}, bf16[576,768]{1,0:T(8,128)(2,1)}, u32[]{:S(2)}) %copy-start) | copy-done | bytes 884760
  2.5 0.0 copy-start.1
  2.5 1.1 %copy-done.1 = bf16[192,2048]{1,0:T(8,128)(2,1)S(1)} copy-done((bf16[192,2048]{1,0:T(8,128)(2,1)S(1)}, bf16[192,2048]{1,0:T(8,128)(2,1)}, u32[]{:S(2)}) %copy-start.1) | copy-done | bytes 786456
  3.6 0.0 copy-start.2
  3.6 1.1 %copy-done.2 = bf16[1,192,2048]{2,1,0:T(8,128)(2,1)S(1)} copy-done((bf16[1,192,2048]{2,1,0:T(8,128)(2,1)S(1)}, bf16[1,192,2048]{2,1,0:T(8,128)(2,1)}, u32[]{:S(2)}) %copy-start.2) | copy-done | bytes 786456
  4.7 0.0 copy-start.3
  4.7 0.7 copy-done.3
  5.4 67.7 %shard_map.76 = (bf16[8,72,768]{2,1,0:T(8,128)(2,1)S(1)}, f32[192,2048]{1,0:T(8,128)S(1)}, f32[2,192]{1,0:T(2,128)S(1)}) custom-call(bf16[192,2048]{1,0:T(8,128)(2,1)S(1)} %copy-done.1, s32[2,192]{1,0:T(2,128)S(1)} %bitcast.13, f32[2,192]{1,0:T(2,128)S(1)} %convert_bitcast_fusion.weights_ref, bf16[8,72,768]{2,1,0:T(8,128)(2,1)S(1)} %bitcast.11, ...), custom_call_target="tpu_custom_call" | custom-call | flops 3623878656 | bytes 8388608 | tf_op jit(solution)/shard_map/pallas_call | solution.py:286
  73.1 0.9 %copy.11 = bf16[576,768]{1,0:T(8,128)(2,1)} copy(bf16[576,768]{1,0:T(8,128)(2,1)S(1)} %bitcast.9) | data formatting | bytes 1769472
  74.0 1.1 %copy.12 = f32[1,192,2048]{2,1,0:T(8,128)} copy(f32[1,192,2048]{2,1,0:T(8,128)S(1)} %bitcast.8) | data formatting | bytes 3145728
  75.2 0.6 copy.13
Async XLA Ops:
  1.3 1.2 %copy-start = (bf16[576,768]{1,0:T(8,128)(2,1)S(1)}, bf16[576,768]{1,0:T(8,128)(2,1)}, u32[]{:S(2)}) copy-start(bf16[576,768]{1,0:T(8,128)(2,1)} %param.8) | copy-start | bytes 2654212
  2.5 1.1 %copy-start.1 = (bf16[192,2048]{1,0:T(8,128)(2,1)S(1)}, bf16[192,2048]{1,0:T(8,128)(2,1)}, u32[]{:S(2)}) copy-start(bf16[192,2048]{1,0:T(8,128)(2,1)} %grad_ref.1) | copy-start | bytes 2359300
  3.6 1.1 %copy-start.2 = (bf16[1,192,2048]{2,1,0:T(8,128)(2,1)S(1)}, bf16[1,192,2048]{2,1,0:T(8,128)(2,1)}, u32[]{:S(2)}) copy-start(bf16[1,192,2048]{2,1,0:T(8,128)(2,1)} %param.9) | copy-start | bytes 2359300
  4.7 0.7 copy-start.3

commit v5 on v4

--- a/solution.py
+++ b/solution.py
@@ -225,12 +225,12 @@
             share = jnp.dot(hid[...], weighted, preferred_element_type=F32)
             part[2 * c + h] = share.astype(BF16).reshape(n_dp, depth, sub)
             red_start(2 * c + h, h)
-        product = jnp.zeros(unscaled.shape, F32)
         for h in range(2):
             mat_wait(2 * c + h, h)
-            product += lax.dot_general(
-                halves[h].astype(BF16), full[2 * c + h].reshape(n_dp * depth, sub),
-                (((1,), (1,)), ((), ())), preferred_element_type=F32)
+        product = lax.dot_general(
+            jnp.concatenate(halves, axis=1).astype(BF16),
+            jnp.concatenate([full[2 * c + h].reshape(n_dp * depth, sub) for h in range(2)], axis=1),
+            (((1,), (1,)), ((), ())), preferred_element_type=F32)
 
         @pl.when(c == 0)
         def _():

time: 76.9 us -> 77 us (level)
  no operation moved by 1% of the time
where the time goes in v5:
time: 77 us; the launch traced here: 75.9 us
  Pallas kernels  67.9 us (88%)
  local copies, waits for them, and re-layouts  6.75 us (9%)
    pallas_call x1, Pallas kernels, per_device(): pl.pallas_call(functools.partial(kernel, n_dp, n_ex, chunks), out_shape=(...  67.9 us
    unnamed x11, local copies, waits for them, and re-layouts  6.75 us

profile of v5, /device:TPU:11, one launch (start us, length us, event | category | flops | bytes accessed | tf_op | source)
XLA Modules:
  0.0 75.9 jit_solution(4998029340673118479)
XLA Ops:
  0.6 0.7 convert_bitcast_fusion.weights_ref
  1.3 0.0 copy-start
  1.3 1.2 %copy-done = bf16[576,768]{1,0:T(8,128)(2,1)S(1)} copy-done((bf16[576,768]{1,0:T(8,128)(2,1)S(1)}, bf16[576,768]{1,0:T(8,128)(2,1)}, u32[]{:S(2)}) %copy-start) | copy-done | bytes 884760
  2.5 0.0 copy-start.1
  2.5 1.1 %copy-done.1 = bf16[192,2048]{1,0:T(8,128)(2,1)S(1)} copy-done((bf16[192,2048]{1,0:T(8,128)(2,1)S(1)}, bf16[192,2048]{1,0:T(8,128)(2,1)}, u32[]{:S(2)}) %copy-start.1) | copy-done | bytes 786456
  3.6 0.0 copy-start.2
  3.6 1.1 %copy-done.2 = bf16[1,192,2048]{2,1,0:T(8,128)(2,1)S(1)} copy-done((bf16[1,192,2048]{2,1,0:T(8,128)(2,1)S(1)}, bf16[1,192,2048]{2,1,0:T(8,128)(2,1)}, u32[]{:S(2)}) %copy-start.2) | copy-done | bytes 786456
  4.7 0.0 copy-start.3
  4.7 0.7 copy-done.3
  5.4 67.9 %shard_map.76 = (bf16[8,72,768]{2,1,0:T(8,128)(2,1)S(1)}, f32[192,2048]{1,0:T(8,128)S(1)}, f32[2,192]{1,0:T(2,128)S(1)}) custom-call(bf16[192,2048]{1,0:T(8,128)(2,1)S(1)} %copy-done.1, s32[2,192]{1,0:T(2,128)S(1)} %bitcast.13, f32[2,192]{1,0:T(2,128)S(1)} %convert_bitcast_fusion.weights_ref, bf16[8,72,768]{2,1,0:T(8,128)(2,1)S(1)} %bitcast.11, ...), custom_call_target="tpu_custom_call" | custom-call | flops 3623878656 | bytes 8388608 | tf_op jit(solution)/shard_map/pallas_call | solution.py:286
  73.3 0.9 %copy.11 = bf16[576,768]{1,0:T(8,128)(2,1)} copy(bf16[576,768]{1,0:T(8,128)(2,1)S(1)} %bitcast.9) | data formatting | bytes 1769472
  74.2 1.1 %copy.12 = f32[1,192,2048]{2,1,0:T(8,128)} copy(f32[1,192,2048]{2,1,0:T(8,128)S(1)} %bitcast.8) | data formatting | bytes 3145728
  75.3 0.6 copy.13
Async XLA Ops:
  1.3 1.2 %copy-start = (bf16[576,768]{1,0:T(8,128)(2,1)S(1)}, bf16[576,768]{1,0:T(8,128)(2,1)}, u32[]{:S(2)}) copy-start(bf16[576,768]{1,0:T(8,128)(2,1)} %param.8) | copy-start | bytes 2654212
  2.5 1.1 %copy-start.1 = (bf16[192,2048]{1,0:T(8,128)(2,1)S(1)}, bf16[192,2048]{1,0:T(8,128)(2,1)}, u32[]{:S(2)}) copy-start(bf16[192,2048]{1,0:T(8,128)(2,1)} %grad_ref.1) | copy-start | bytes 2359300
  3.6 1.1 %copy-start.2 = (bf16[1,192,2048]{2,1,0:T(8,128)(2,1)S(1)}, bf16[1,192,2048]{2,1,0:T(8,128)(2,1)}, u32[]{:S(2)}) copy-start(bf16[1,192,2048]{2,1,0:T(8,128)(2,1)} %param.9) | copy-start | bytes 2359300
  4.7 0.7 copy-start.3
